TPU v7x, 32 devices: a whole 2x2x4 slice. The times are simulated.
32 devices in a mesh: harm: 4 (over z), node: 8 (over y, x, core).
Axes of the slice: x: 2, y: 2, z: 4, core: 2. Of those that a mesh axis runs over, the one named last changes fastest.
Arguments:
- adjoint: bfloat16 [128, 4, 32768], P('harm', None, 'node'), may hold values from -6 to 6
- source: float32 [128, 131072], P(None, ('harm', 'node')), may hold values from -6 to 6
- rad_coeff: bfloat16 [128, 131072], P(None, ('harm', 'node')), may hold values from 0.19921875 to 2
- capacity: float32 [131072], P(('harm', 'node')), may hold values from 0.005 to 0.03
- inv_diag: float32 [131072], P(('harm', 'node')), may hold values from 0.1 to 0.5
- blocks: bfloat16 [1024, 4, 128, 128], P(('harm', 'node')), may hold values from -0.25 to 0.25
- block_cols: int32 [1024, 4], P(('harm', 'node')), may hold values from 0 to 1023, as said below
- zone_of: int32 [131072], P(('harm', 'node')), may hold values from 0 to 1279, as said below
- heater_weight: float32 [131072], P(('harm', 'node')), may hold values from 0.2 to 2
Outputs:
- updated: bfloat16 [128, 4, 32768], P('harm', None, 'node')
- gradient: float32 [1280, 128], P(('harm', 'node'))
Inputs may be any that keep to these rules, and one draw needn't show every extreme that they name: `block_cols`: with d = b // 32 and D = 32: slot 0 of row block b names b itself; slot 1 lies in row blocks max(d - 1, 0) * 32 to (max(d - 1, 0) + 1) * 32 - 1; slot 2 in min(d + 1, D - 1) * 32 to (min(d + 1, D - 1) + 1) * 32 - 1; the other slots in (d - 1) * 32 to (d + 2) * 32 - 1. `zone_of`: node n lies in a zone z with (n // 4096 - 1) * 40 <= z < (n // 4096 + 2) * 40.
All inputs are finite; a program needn't handle non-finite values.
Results may differ from a plain program's by a relative error of at most 0.0035.
Values may be sent and summed in bfloat16 or wider, within the bound.
A program may use at most 64 MiB of HBM per device.

v0:
```python
import math
import jax
import jax.numpy as jnp
from jax import lax
from jax.sharding import PartitionSpec as P

ZONE_DEV = 40


def with_halo(value, sides, width):
    for axis, dim in sides:
        count, length = (lax.axis_size(axis), value.shape[dim])
        up = [(i, (i + 1) % count) for i in range(count - 1)]
        down = [(j, i) for i, j in up]
        last = lax.slice_in_dim(value, length - width, length, axis=dim)
        initial = lax.slice_in_dim(value, 0, width, axis=dim)
        before = lax.ppermute(last, axis, up)
        after = lax.ppermute(initial, axis, down)
        value = jnp.concatenate([before, value, after], axis=dim)
    return value


def passed_along(value, axis, steps):
    count = lax.axis_size(axis)
    initial, last = (max(0, -steps), min(count, count - steps))
    return lax.ppermute(value, axis, [(source, source + steps) for source in range(initial, last)])


def fourier_basis(count):
    sample_index = jnp.arange(count, dtype=jnp.float32)[:, None]
    column_index = jnp.arange(count)[None, :]
    half_count = count // 2
    frequency = jnp.where(
        column_index <= half_count, column_index, column_index - half_count
    ).astype(jnp.float32)
    angle = 2.0 * math.pi * frequency * sample_index / count
    values_table = jnp.where(column_index <= half_count, jnp.cos(angle), jnp.sin(angle))
    scaling = jnp.where(
        (column_index == 0) | (column_index == half_count),
        math.sqrt(1.0 / count),
        math.sqrt(2.0 / count),
    )
    return (values_table * scaling).astype(jnp.bfloat16)


def derivative_term(field):
    half_count = field.shape[0] // 2
    wave_number = jnp.arange(1, half_count, dtype=jnp.float32)[:, None]
    zero_row = jnp.zeros((1, field.shape[1]), jnp.float32)
    upper_rows = wave_number * field[half_count + 1 :]
    lower_rows = -wave_number * field[1:half_count]
    return jnp.concatenate([zero_row, upper_rows, zero_row, lower_rows], axis=0)


def body(
    adjoint, source, rad_coeff, capacity, inv_diag, blocks, block_cols, zone_of, heater_weight
):
    arrived = lax.all_to_all(adjoint, "harm", split_axis=1, concat_axis=0, tiled=True)
    harmonics = arrived.shape[0]
    node_count = arrived.shape[2]
    field = arrived.reshape(harmonics, node_count)
    block_size = blocks.shape[2]
    row_blocks = node_count // block_size
    fourier = fourier_basis(harmonics)
    samples = jnp.dot(fourier, field, preferred_element_type=jnp.float32)
    weighted = (rad_coeff.astype(jnp.float32) * samples).astype(jnp.bfloat16)
    radiative = jnp.dot(fourier.T, weighted, preferred_element_type=jnp.float32)
    rate_term = derivative_term(field.astype(jnp.float32))
    padded = with_halo(field, ((("harm", "node"), 1),), node_count)
    position = lax.axis_index(("harm", "node"))
    local_cols = block_cols - (position - 1) * row_blocks
    extended = padded.reshape(harmonics, 3 * row_blocks, block_size)
    gathered = jnp.take(extended, local_cols, axis=1)
    conduction = jnp.einsum(
        "kbsj,bsij->kbi", gathered, blocks, preferred_element_type=jnp.float32
    ).reshape(harmonics, node_count)
    residual = source - (capacity[None, :] * rate_term + conduction + radiative)
    updated = (field.astype(jnp.float32) + inv_diag[None, :] * residual).astype(jnp.bfloat16)
    returned = lax.all_to_all(
        updated.reshape(harmonics, 1, node_count), "harm", split_axis=0, concat_axis=1, tiled=True
    )
    weighted_terms = (updated.astype(jnp.float32) * heater_weight[None, :]).T
    window_zone = zone_of - (position - 1) * ZONE_DEV
    selector = (window_zone[:, None] == jnp.arange(3 * ZONE_DEV, dtype=jnp.int32)[None, :]).astype(
        jnp.float32
    )
    window_sums = jnp.einsum("nz,nk->zk", selector, weighted_terms, precision=lax.Precision.HIGHEST)
    lower_part = window_sums[:ZONE_DEV]
    middle_part = window_sums[ZONE_DEV : 2 * ZONE_DEV]
    upper_part = window_sums[2 * ZONE_DEV :]
    above_terms = passed_along(lower_part, ("harm", "node"), -1)
    below_terms = passed_along(upper_part, ("harm", "node"), 1)
    gradient = middle_part + above_terms + below_terms
    return (returned, gradient)


def solution(mesh):
    in_specs = (
        P("harm", None, "node"),
        P(None, ("harm", "node")),
        P(None, ("harm", "node")),
        P(("harm", "node")),
        P(("harm", "node")),
        P(("harm", "node"), None, None, None),
        P(("harm", "node"), None),
        P(("harm", "node")),
        P(("harm", "node")),
    )
    out_specs = (P("harm", None, "node"), P(("harm", "node"), None))
    return jax.shard_map(body, mesh=mesh, in_specs=in_specs, out_specs=out_specs, check_vma=False)
```

profile of v0, /device:TPU:4, one launch (start us, length us, event | category | flops | bytes accessed | tf_op | source)
XLA Modules:
  0.0 116.6 jit_solution(15993468261064862405)
XLA Ops:
  0.6 0.0 copy-start.6
  0.6 2.8 %copy.35 = bf16[32,4,4096]{2,0,1:T(8,128)(2,1)} copy(bf16[32,4,4096]{2,1,0:T(4,128)(2,1)} %param.9) | data formatting | bytes 2097152 | tf_op args[0]
  3.4 4.9 %all-to-all-start = ((bf16[32,4,4096]{2,0,1:T(8,128)(2,1)}), bf16[32,4,4096]{2,0,1:T(8,128)(2,1)S(1)}, u32[]{:S(2)}, u32[]{:S(2)}) async-start(bf16[32,4,4096]{2,0,1:T(8,128)(2,1)} %copy.35), calls=%async_computation | async-start | bytes 2097152 | tf_op jit(solution)/shard_map/all_to_all | solution.py:58
  8.3 0.0 copy-done.6
  8.3 0.1 copy.40
  8.4 0.1 reshape.72
  8.5 0.1 copy.36
  8.6 25.4 %all-to-all-done = bf16[32,4,4096]{2,0,1:T(8,128)(2,1)S(1)} async-done(((bf16[32,4,4096]{2,0,1:T(8,128)(2,1)}), bf16[32,4,4096]{2,0,1:T(8,128)(2,1)S(1)}, u32[]{:S(2)}, u32[]{:S(2)}) %all-to-all-start) | async-done | bytes 1048608 | tf_op jit(solution)/shard_map/all_to_all | solution.py:58
  34.0 0.0 copy-start
  34.0 2.0 %collective-permute-start.1 = (bf16[128,4096]{1,0:T(8,128)(2,1)S(1)}, bf16[128,4096]{1,0:T(8,128)(2,1)S(1)}, u32[]{:S(2)}, u32[]{:S(2)}) collective-permute-start(bf16[128,4096]{1,0:T(8,128)(2,1)S(1)} %bitcast.39), channel_id=1, source_target_pairs={{1,0},{2,1},{3,2},{4,3},{5,4},{6,5},{7,6},{8,7},{9,8},{10,9},{11,1... | collective-permute-start | bytes 3145736 | tf_op jit(solution)/shard_map/ppermute | solution.py:18
  36.0 2.3 %collective-permute-start = (bf16[128,4096]{1,0:T(8,128)(2,1)S(1)}, bf16[128,4096]{1,0:T(8,128)(2,1)S(1)}, u32[]{:S(2)}, u32[]{:S(2)}) collective-permute-start(bf16[128,4096]{1,0:T(8,128)(2,1)S(1)} %bitcast.40), channel_id=1, source_target_pairs={{0,1},{1,2},{2,3},{3,4},{4,5},{5,6},{6,7},{7,8},{8,9},{9,10},{10,1... | collective-permute-start | bytes 3145736 | tf_op jit(solution)/shard_map/ppermute | solution.py:17
  38.3 0.3 bitcast_convert_fusion
  38.6 0.2 copy.48
  38.9 0.0 copy-done
  38.9 0.4 copy.38
  39.3 1.6 %slice_multiply_fusion.1 = (f32[63,4096]{1,0:T(8,128)}, f32[63,4096]{1,0:T(8,128)}) fusion(f32[128,4096]{1,0:T(8,128)S(1)} %bitcast_convert_fusion, f32[63]{0:T(128)S(1)} %get-tuple-element.10, f32[63]{0:T(128)S(1)} %get-tuple-element.11), kind=kLoop, calls=%fused_computation.24 | loop fusion | flops 516096 | bytes 4129272 | tf_op jit(solution)/shard_map/mul | solution.py:50
  40.9 15.8 %collective-permute-done.1 = bf16[128,4096]{1,0:T(8,128)(2,1)S(1)} collective-permute-done((bf16[128,4096]{1,0:T(8,128)(2,1)S(1)}, bf16[128,4096]{1,0:T(8,128)(2,1)S(1)}, u32[]{:S(2)}, u32[]{:S(2)}) %collective-permute-start.1) | collective-permute-done | bytes 1048608 | tf_op jit(solution)/shard_map/ppermute | solution.py:18
  56.7 0.3 copy_bitcast_fusion
  57.0 4.3 %collective-permute-done = bf16[128,4096]{1,0:T(8,128)(2,1)S(1)} collective-permute-done((bf16[128,4096]{1,0:T(8,128)(2,1)S(1)}, bf16[128,4096]{1,0:T(8,128)(2,1)S(1)}, u32[]{:S(2)}, u32[]{:S(2)}) %collective-permute-start) | collective-permute-done | bytes 1048608 | tf_op jit(solution)/shard_map/ppermute | solution.py:17
  61.4 0.3 copy_bitcast_fusion.1
  61.6 0.4 pad_maximum_fusion
  62.0 3.0 %gather_fusion = bf16[128,128,128]{2,1,0:T(8,128)(2,1)} fusion(bf16[128,96,128]{2,0,1:T(8,128)(2,1)S(1)} %pad_maximum_fusion, s32[1024]{0:T(1024)S(1)} %pad_clamp_fusion), kind=kCustom, calls=%fused_computation | custom fusion | bytes 8389120 | tf_op jit(solution)/shard_map/jit(_take)/gather | solution.py:73
  65.1 6.2 %fusion.5 = f32[32,128,128,1]{1,2,3,0:T(8,128)} fusion(bf16[32,4,128,128]{3,2,1,0:T(8,128)(2,1)} %param.14, bf16[32,4,128,128]{3,2,1,0:T(8,128)(2,1)} %bitcast.44, pred[32,4]{1,0:T(8,128)(4,1)S(1)} %copy.36), kind=kOutput, calls=%fused_computation.8 | convolution fusion | flops 538968064 | bytes 10485888 | tf_op jit(solution)/shard_map/kbsj,bsij->kbi/dot_general | solution.py:74
  71.3 0.0 copy-start.1
  71.3 0.0 copy-start.3
  71.3 0.0 copy-start.4
  71.3 2.0 %copy.41 = f32[128,4096]{1,0:T(8,128)S(1)} copy(f32[128,4096]{0,1:T(8,128)} %bitcast.47) | data formatting | bytes 4194304 | tf_op jit(solution)/shard_map/reshape | solution.py:76
  73.3 0.0 copy-done.1
  73.3 0.0 copy-done.3
  73.3 0.0 copy-done.4
  73.3 5.2 %fusion.4 = bf16[128,4096]{1,0:T(8,128)(2,1)} fusion(f32[128,4096]{1,0:T(8,128)} %param.10, f32[128,4096]{1,0:T(8,128)S(1)} %copy.41, f32[63,4096]{1,0:T(8,128)} %get-tuple-element.7, f32[1,4096]{1,0:T(1,128)S(1)} %broadcast_in_dim.41, f32[63,4096]{1,0:T(8,128)} %get-tuple-element.6, bf16[128,4096]{1,0:T(8,128)(2,1)S(1)} %bitcast.42, ...), kind=kOutput, calls=%fused_computation.7 | convolution fusion | flops 275939328 | bytes 9454720 | tf_op jit(solution)/shard_map/dot_general | solution.py:67
  78.5 0.5 broadcast.81
  79.0 2.6 %reduce = bf16[128,4096]{1,0:T(8,128)(2,1)S(1)} reduce(bf16[128,1,4096]{2,0,1:T(8,128)(2,1)} %bitcast.46, bf16[]{:T(256)} %broadcast.81), dimensions={1}, to_apply=%copy.42.reduce_sub_computation | reduce | bytes 2097154 | tf_op jit(solution)/shard_map/reshape | solution.py:80
  81.7 0.0 copy-start.5
  81.7 0.0 copy-start.2
  81.7 0.0 copy-start.7
  81.7 2.0 %reshape.81 = bf16[4,2,65536]{2,1,0:T(2,128)(2,1)} reshape(bf16[128,4096]{1,0:T(8,128)(2,1)S(1)} %reduce) | data formatting | bytes 2097152
  83.7 3.5 %all-to-all-start.1 = ((bf16[4,2,65536]{2,1,0:T(2,128)(2,1)}), bf16[4,2,65536]{2,1,0:T(2,128)(2,1)S(1)}, u32[]{:S(2)}, u32[]{:S(2)}) async-start(bf16[4,2,65536]{2,1,0:T(2,128)(2,1)} %reshape.81), calls=%async_computation.1 | async-start | bytes 2097152 | tf_op jit(solution)/shard_map/all_to_all | solution.py:79
  87.2 0.0 copy-done.5
  87.2 0.0 copy-done.2
  87.3 0.0 copy-done.7
  87.3 2.1 %fusion.11 = f32[120,128]{1,0:T(8,128)S(1)} fusion(bf16[128,4096]{1,0:T(8,128)(2,1)S(1)} %copy-done.2, f32[4096]{0:T(1024)S(1)} %copy-done.7, s32[4096]{0:T(1024)S(1)} %broadcast_subtract_fusion), kind=kOutput, calls=%fused_computation.16 | convolution fusion | flops 757006336 | bytes 1142784 | tf_op jit(solution)/shard_map/nz,nk->zk/dot_general | solution.py:87
  89.4 1.9 %collective-permute-start.2 = (f32[40,128]{1,0:T(8,128)S(1)}, f32[40,128]{1,0:T(8,128)S(1)}, u32[]{:S(2)}, u32[]{:S(2)}) collective-permute-start(f32[40,128]{1,0:T(8,128)S(1)} %get-tuple-element.8), channel_id=1, source_target_pairs={{1,0},{2,1},{3,2},{4,3},{5,4},{6,5},{7,6},{8,7},{9,8},{10,9},{11,1... | collective-permute-start | bytes 61448 | tf_op jit(solution)/shard_map/ppermute | solution.py:26
  91.3 2.4 %collective-permute-start.3 = (f32[40,128]{1,0:T(8,128)S(1)}, f32[40,128]{1,0:T(8,128)S(1)}, u32[]{:S(2)}, u32[]{:S(2)}) collective-permute-start(f32[40,128]{1,0:T(8,128)S(1)} %get-tuple-element.9), channel_id=1, source_target_pairs={{0,1},{1,2},{2,3},{3,4},{4,5},{5,6},{6,7},{7,8},{8,9},{9,10},{10,1... | collective-permute-start | bytes 61448 | tf_op jit(solution)/shard_map/ppermute | solution.py:26
  93.7 0.0 collective-permute-done.2
  93.7 3.6 %collective-permute-done.3 = f32[40,128]{1,0:T(8,128)S(1)} collective-permute-done((f32[40,128]{1,0:T(8,128)S(1)}, f32[40,128]{1,0:T(8,128)S(1)}, u32[]{:S(2)}, u32[]{:S(2)}) %collective-permute-start.3) | collective-permute-done | bytes 20512 | tf_op jit(solution)/shard_map/ppermute | solution.py:26
  97.3 0.6 fusion.26
  97.9 14.8 %all-to-all-done.1 = bf16[4,2,65536]{2,1,0:T(2,128)(2,1)S(1)} async-done(((bf16[4,2,65536]{2,1,0:T(2,128)(2,1)}), bf16[4,2,65536]{2,1,0:T(2,128)(2,1)S(1)}, u32[]{:S(2)}, u32[]{:S(2)}) %all-to-all-start.1) | async-done | bytes 1048608 | tf_op jit(solution)/shard_map/all_to_all | solution.py:79
  112.7 0.9 reshape.82
  113.7 1.1 copy.45
  114.9 1.8 %copy.43 = bf16[32,4,4096]{2,1,0:T(4,128)(2,1)} copy(bf16[32,4,4096]{2,0,1:T(8,128)(2,1)S(1)} %bitcast.43) | data formatting | bytes 2097152
  (8 shorter events, 0.1 us)
Async XLA Ops:
  0.6 7.7 %copy-start.6 = (s32[32,4]{0,1:T(4,128)S(1)}, s32[32,4]{0,1:T(4,128)}, u32[]{:S(2)}) copy-start(s32[32,4]{0,1:T(4,128)} %param.15) | copy-start | bytes 1540
  3.4 30.6 %all-to-all-start = ((bf16[32,4,4096]{2,0,1:T(8,128)(2,1)}), bf16[32,4,4096]{2,0,1:T(8,128)(2,1)S(1)}, u32[]{:S(2)}, u32[]{:S(2)}) async-start(bf16[32,4,4096]{2,0,1:T(8,128)(2,1)} %copy.35), calls=%async_computation | async-start | bytes 2097152 | tf_op jit(solution)/shard_map/all_to_all | solution.py:58
  34.0 4.9 %copy-start = (bf16[32,4,4096]{2,0,1:T(8,128)(2,1)}, bf16[32,4,4096]{2,0,1:T(8,128)(2,1)S(1)}, u32[]{:S(2)}) copy-start(bf16[32,4,4096]{2,0,1:T(8,128)(2,1)S(1)} %all-to-all-done) | copy-start | bytes 3145732
  34.0 22.7 %collective-permute-start.1 = (bf16[128,4096]{1,0:T(8,128)(2,1)S(1)}, bf16[128,4096]{1,0:T(8,128)(2,1)S(1)}, u32[]{:S(2)}, u32[]{:S(2)}) collective-permute-start(bf16[128,4096]{1,0:T(8,128)(2,1)S(1)} %bitcast.39), channel_id=1, source_target_pairs={{1,0},{2,1},{3,2},{4,3},{5,4},{6,5},{7,6},{8,7},{9,8},{10,9},{11,1... | collective-permute-start | bytes 3145736 | tf_op jit(solution)/shard_map/ppermute | solution.py:18
  36.0 25.3 %collective-permute-start = (bf16[128,4096]{1,0:T(8,128)(2,1)S(1)}, bf16[128,4096]{1,0:T(8,128)(2,1)S(1)}, u32[]{:S(2)}, u32[]{:S(2)}) collective-permute-start(bf16[128,4096]{1,0:T(8,128)(2,1)S(1)} %bitcast.40), channel_id=1, source_target_pairs={{0,1},{1,2},{2,3},{3,4},{4,5},{5,6},{6,7},{7,8},{8,9},{9,10},{10,1... | collective-permute-start | bytes 3145736 | tf_op jit(solution)/shard_map/ppermute | solution.py:17
  71.3 2.0 %copy-start.1 = (bf16[32,4,4096]{2,0,1:T(8,128)(2,1)S(1)}, bf16[32,4,4096]{2,0,1:T(8,128)(2,1)}, u32[]{:S(2)}) copy-start(bf16[32,4,4096]{2,0,1:T(8,128)(2,1)} %copy-done) | copy-start | bytes 3145732
  71.3 2.0 %copy-start.3 = (f32[4096]{0:T(1024)S(1)}, f32[4096]{0:T(1024)}, u32[]{:S(2)}) copy-start(f32[4096]{0:T(1024)} %param.12) | copy-start | bytes 49156
  71.3 2.1 %copy-start.4 = (f32[4096]{0:T(1024)S(1)}, f32[4096]{0:T(1024)}, u32[]{:S(2)}) copy-start(f32[4096]{0:T(1024)} %param.13) | copy-start | bytes 49156
  81.7 5.6 %copy-start.5 = (s32[4096]{0:T(1024)S(1)}, s32[4096]{0:T(1024)}, u32[]{:S(2)}) copy-start(s32[4096]{0:T(1024)} %param.16) | copy-start | bytes 49156
  81.7 5.6 %copy-start.2 = (bf16[128,4096]{1,0:T(8,128)(2,1)S(1)}, bf16[128,4096]{1,0:T(8,128)(2,1)}, u32[]{:S(2)}) copy-start(bf16[128,4096]{1,0:T(8,128)(2,1)} %fusion.4) | copy-start | bytes 3145732
  81.7 5.6 %copy-start.7 = (f32[4096]{0:T(1024)S(1)}, f32[4096]{0:T(1024)}, u32[]{:S(2)}) copy-start(f32[4096]{0:T(1024)} %param.17) | copy-start | bytes 49156
  83.7 29.0 %all-to-all-start.1 = ((bf16[4,2,65536]{2,1,0:T(2,128)(2,1)}), bf16[4,2,65536]{2,1,0:T(2,128)(2,1)S(1)}, u32[]{:S(2)}, u32[]{:S(2)}) async-start(bf16[4,2,65536]{2,1,0:T(2,128)(2,1)} %reshape.81), calls=%async_computation.1 | async-start | bytes 2097152 | tf_op jit(solution)/shard_map/all_to_all | solution.py:79
  89.4 4.3 %collective-permute-start.2 = (f32[40,128]{1,0:T(8,128)S(1)}, f32[40,128]{1,0:T(8,128)S(1)}, u32[]{:S(2)}, u32[]{:S(2)}) collective-permute-start(f32[40,128]{1,0:T(8,128)S(1)} %get-tuple-element.8), channel_id=1, source_target_pairs={{1,0},{2,1},{3,2},{4,3},{5,4},{6,5},{7,6},{8,7},{9,8},{10,9},{11,1... | collective-permute-start | bytes 61448 | tf_op jit(solution)/shard_map/ppermute | solution.py:26
  91.3 6.0 %collective-permute-start.3 = (f32[40,128]{1,0:T(8,128)S(1)}, f32[40,128]{1,0:T(8,128)S(1)}, u32[]{:S(2)}, u32[]{:S(2)}) collective-permute-start(f32[40,128]{1,0:T(8,128)S(1)} %get-tuple-element.9), channel_id=1, source_target_pairs={{0,1},{1,2},{2,3},{3,4},{4,5},{5,6},{6,7},{7,8},{8,9},{9,10},{10,1... | collective-permute-start | bytes 61448 | tf_op jit(solution)/shard_map/ppermute | solution.py:26
where the time goes:
time: 117 us
  waiting for transfers between devices  63.9 us (55%)
  starting transfers between devices  17 us (15%)
  local copies, waits for them, and re-layouts  15.8 us (14%)
  matrix products  13.5 us (12%)
  other arithmetic  5.56 us (5%)
    all_to_all x1, waiting for transfers between devices, body(): lax.all_to_all(adjoint, 'harm', split_axis=1, concat_axis=0, tiled=True)  25.4 us
    ppermute x1, waiting for transfers between devices, with_halo(): after = lax.ppermute(initial, axis, down)  15.8 us
    all_to_all x1, waiting for transfers between devices, body(): lax.all_to_all(updated.reshape(harmonics, 1, node_count), 'harm', split_a...  14.8 us
    unnamed x22, local copies, waits for them, and re-layouts  8.93 us
    dot_general x1, matrix products, body(): jnp.einsum('kbsj,bsij->kbi', gathered, blocks, preferred_element_type=jnp...  6.17 us
    dot_general x1, matrix products, body(): radiative = jnp.dot(fourier.T, weighted, preferred_element_type=jnp.float32)  5.2 us
    all_to_all x1, starting transfers between devices, body(): lax.all_to_all(adjoint, 'harm', split_axis=1, concat_axis=0, tiled=True)  4.87 us
    ppermute x2, starting transfers between devices, passed_along(): lax.ppermute(value, axis, [(source, source + steps) for source in range(i...  4.33 us
  transfers between devices with their start and end apart: 6, of which 5 were waited for; matrix products, arithmetic and copies ran while one was open for 5% of the time, Pallas kernels for 0%

commit v1 on v0

--- a/solution.py
+++ b/solution.py
@@ -5,6 +5,18 @@
 from jax.sharding import PartitionSpec as P
 
 ZONE_DEV = 40
+
+
+def carry_matrix(chunk, axis_no, w_in):
+    current_arr, seen_now = (chunk.shape[:axis_no], chunk.shape[axis_no + 1 :])
+    odd = chunk.reshape(*current_arr, w_in, -1, *seen_now)
+    return jnp.moveaxis(odd, axis_no, 0)
+
+
+def rails_balance(view, ndim_at):
+    a_next = list(view.shape[1:])
+    a_next[ndim_at] *= view.shape[0]
+    return jnp.moveaxis(view, 0, ndim_at).reshape(a_next)
 
 
 def with_halo(value, sides, width):
@@ -55,7 +67,18 @@
 def body(
     adjoint, source, rad_coeff, capacity, inv_diag, blocks, block_cols, zone_of, heater_weight
 ):
-    arrived = lax.all_to_all(adjoint, "harm", split_axis=1, concat_axis=0, tiled=True)
+    y1 = lax.axis_index("harm")
+    d_next = lax.axis_size("harm")
+    mid_arr, top = (d_next, y1)
+    all_rows = carry_matrix(adjoint, 1, mid_arr)
+    blocks_here = [all_rows[top]]
+    for s in [*range(1, mid_arr)]:
+        w_next = all_rows[top ^ s]
+        blocks_here.append(
+            lax.ppermute(w_next, axis_name="harm", perm=[(h, h ^ s) for h in range(mid_arr)])
+        )
+    all_rows = jnp.stack(blocks_here)[top ^ jnp.arange(mid_arr)]
+    arrived = rails_balance(all_rows, 0)
     harmonics = arrived.shape[0]
     node_count = arrived.shape[2]
     field = arrived.reshape(harmonics, node_count)

time: 117 us -> 117 us (level)
  waiting for transfers between devices: 63.9 us -> 56.9 us
  local copies, waits for them, and re-layouts: 15.8 us -> 19.8 us
  starting transfers between devices: 17 us -> 20.3 us
    all_to_all x1 -> x0, waiting for transfers between devices: 25.4 us -> none  [body(): lax.all_to_all(adjoint, 'harm', split_axis=1, concat_axis=0, tiled=True)]
    ppermute x0 -> x3, waiting for transfers between devices: none -> 17.5 us  [body(): lax.ppermute(w_next, axis_name='harm', perm=[(h, h ^ s) for h in range(mi...]
    another operation x0 -> x1, local copies, waits for them, and re-layouts: none -> 5.07 us
    all_to_all x1 -> x0, starting transfers between devices: 4.87 us -> none  [body(): lax.all_to_all(adjoint, 'harm', split_axis=1, concat_axis=0, tiled=True)]
    ppermute x0 -> x3, starting transfers between devices: none -> 4.58 us  [body(): lax.ppermute(w_next, axis_name='harm', perm=[(h, h ^ s) for h in range(mi...]
    all_to_all x1, starting transfers between devices: 3.52 us -> 7.02 us  [body(): lax.all_to_all(updated.reshape(harmonics, 1, node_count), 'harm', split_a...]
    unnamed x22 -> x25, local copies, waits for them, and re-layouts: 8.93 us -> 7.32 us
  transfers between devices with their start and end apart: 6 -> 8, of which waited for: 5 -> 6; matrix products, arithmetic and copies ran while one was open for 5% -> 6% of each run, Pallas kernels for 0% -> 0%
where the time goes in v1:
time: 117 us
  waiting for transfers between devices  56.9 us (49%)
  starting transfers between devices  20.3 us (17%)
  local copies, waits for them, and re-layouts  19.8 us (17%)
  matrix products  13.5 us (12%)
  other arithmetic  5.7 us (5%)
    ppermute x3, waiting for transfers between devices, body(): lax.ppermute(w_next, axis_name='harm', perm=[(h, h ^ s) for h in range(mi...  17.5 us
    all_to_all x1, waiting for transfers between devices, body(): lax.all_to_all(updated.reshape(harmonics, 1, node_count), 'harm', split_a...  15.7 us
    ppermute x1, waiting for transfers between devices, with_halo(): after = lax.ppermute(initial, axis, down)  15.6 us
    unnamed x25, local copies, waits for them, and re-layouts  7.32 us
    all_to_all x1, starting transfers between devices, body(): lax.all_to_all(updated.reshape(harmonics, 1, node_count), 'harm', split_a...  7.02 us
    dot_general x1, matrix products, body(): jnp.einsum('kbsj,bsij->kbi', gathered, blocks, preferred_element_type=jnp...  6.16 us
    dot_general x1, matrix products, body(): radiative = jnp.dot(fourier.T, weighted, preferred_element_type=jnp.float32)  5.23 us
    another operation x1, local copies, waits for them, and re-layouts  5.07 us
  transfers between devices with their start and end apart: 8, of which 6 were waited for; matrix products, arithmetic and copies ran while one was open for 6% of the time, Pallas kernels for 0%

profile of v1, /device:TPU:4, one launch (start us, length us, event | category | flops | bytes accessed | tf_op | source)
XLA Modules:
  0.0 117.1 jit_solution(4078237222329528995)
XLA Ops:
  0.6 5.1 %constant_dynamic-slice_fusion.3 = (bf16[32,1,4096]{2,1,0:T(2,128)(2,1)S(1)}, bf16[32,1,4096]{2,1,0:T(2,128)(2,1)S(1)}, bf16[32,1,4096]{2,1,0:T(2,128)(2,1)S(1)}, bf16[32,1,4096]{2,1,0:T(2,128)(2,1)S(1)}) fusion(bf16[32,4,4096]{2,1,0:T(4,128)(2,1)} %param.9, s32[]{:T(128)S(6)} %select_n.59, s32[]{:T(128)S(6)} %select_n.61, s32[]{:T(128)S(6)} %select_n.60, ...), kind=kLoop, calls=%fused_computation.47 | loop fusion | bytes 2097168 | tf_op jit(solution)/shard_map/dynamic-slice.4
  5.7 0.0 copy-start.6
  5.7 0.3 copy.66
  6.0 1.6 %collective-permute-start = (bf16[32,1,4096]{2,0,1:T(8,128)(2,1)S(1)}, bf16[32,1,4096]{2,0,1:T(8,128)(2,1)S(1)}, u32[]{:S(2)}, u32[]{:S(2)}) collective-permute-start(bf16[32,1,4096]{2,0,1:T(8,128)(2,1)S(1)} %copy.66), channel_id=1, source_target_pairs={{0,8},{8,0},{16,24},{24,16},{1,9},{9,1},{17,25},{25,17},{2,10},{10... | collective-permute-start | bytes 786440 | tf_op jit(solution)/shard_map/ppermute | solution.py:78
  7.7 0.3 copy.67
  8.0 2.7 %collective-permute-start.1 = (bf16[32,1,4096]{2,0,1:T(8,128)(2,1)S(1)}, bf16[32,1,4096]{2,0,1:T(8,128)(2,1)S(1)}, u32[]{:S(2)}, u32[]{:S(2)}) collective-permute-start(bf16[32,1,4096]{2,0,1:T(8,128)(2,1)S(1)} %copy.67), channel_id=1, source_target_pairs={{0,16},{8,24},{16,0},{24,8},{1,17},{9,25},{17,1},{25,9},{2,18},{10... | collective-permute-start | bytes 786440 | tf_op jit(solution)/shard_map/ppermute | solution.py:78
  10.6 0.3 copy.68
  10.9 0.3 collective-permute-start.2
  11.3 0.0 copy-done.6
  11.3 0.3 copy.75
  11.6 0.1 copy.59
  11.7 0.1 reshape.109
  11.8 0.1 copy.55
  11.9 6.9 %collective-permute-done = bf16[32,1,4096]{2,0,1:T(8,128)(2,1)S(1)} collective-permute-done((bf16[32,1,4096]{2,0,1:T(8,128)(2,1)S(1)}, bf16[32,1,4096]{2,0,1:T(8,128)(2,1)S(1)}, u32[]{:S(2)}, u32[]{:S(2)}) %collective-permute-start) | collective-permute-done | bytes 262176 | tf_op jit(solution)/shard_map/ppermute | solution.py:78
  18.8 10.6 %collective-permute-done.1 = bf16[32,1,4096]{2,0,1:T(8,128)(2,1)S(1)} collective-permute-done((bf16[32,1,4096]{2,0,1:T(8,128)(2,1)S(1)}, bf16[32,1,4096]{2,0,1:T(8,128)(2,1)S(1)}, u32[]{:S(2)}, u32[]{:S(2)}) %collective-permute-start.1) | collective-permute-done | bytes 262176 | tf_op jit(solution)/shard_map/ppermute | solution.py:78
  29.4 0.0 collective-permute-done.2
  29.4 0.1 maximum_bitcast_fusion
  29.5 0.6 gather_fusion
  30.2 0.0 copy-start
  30.2 1.9 %collective-permute-start.4 = (bf16[128,4096]{1,0:T(8,128)(2,1)S(1)}, bf16[128,4096]{1,0:T(8,128)(2,1)S(1)}, u32[]{:S(2)}, u32[]{:S(2)}) collective-permute-start(bf16[128,4096]{1,0:T(8,128)(2,1)S(1)} %bitcast.43), channel_id=1, source_target_pairs={{1,0},{2,1},{3,2},{4,3},{5,4},{6,5},{7,6},{8,7},{9,8},{10,9},{11,1... | collective-permute-start | bytes 3145736 | tf_op jit(solution)/shard_map/ppermute | solution.py:30
  32.1 2.4 %collective-permute-start.3 = (bf16[128,4096]{1,0:T(8,128)(2,1)S(1)}, bf16[128,4096]{1,0:T(8,128)(2,1)S(1)}, u32[]{:S(2)}, u32[]{:S(2)}) collective-permute-start(bf16[128,4096]{1,0:T(8,128)(2,1)S(1)} %bitcast.44), channel_id=1, source_target_pairs={{0,1},{1,2},{2,3},{3,4},{4,5},{5,6},{6,7},{7,8},{8,9},{9,10},{10,1... | collective-permute-start | bytes 3145736 | tf_op jit(solution)/shard_map/ppermute | solution.py:29
  34.5 0.3 bitcast_convert_fusion
  34.8 0.2 copy.71
  35.1 0.0 copy-done
  35.1 0.4 copy.57
  35.5 1.6 %slice_multiply_fusion.1 = (f32[63,4096]{1,0:T(8,128)}, f32[63,4096]{1,0:T(8,128)}) fusion(f32[128,4096]{1,0:T(8,128)S(1)} %bitcast_convert_fusion, f32[63]{0:T(128)S(1)} %get-tuple-element.14, f32[63]{0:T(128)S(1)} %get-tuple-element.15), kind=kLoop, calls=%fused_computation.25 | loop fusion | flops 516096 | bytes 4129272 | tf_op jit(solution)/shard_map/mul | solution.py:62
  37.1 15.6 %collective-permute-done.4 = bf16[128,4096]{1,0:T(8,128)(2,1)S(1)} collective-permute-done((bf16[128,4096]{1,0:T(8,128)(2,1)S(1)}, bf16[128,4096]{1,0:T(8,128)(2,1)S(1)}, u32[]{:S(2)}, u32[]{:S(2)}) %collective-permute-start.4) | collective-permute-done | bytes 1048608 | tf_op jit(solution)/shard_map/ppermute | solution.py:30
  52.7 0.3 copy_bitcast_fusion
  53.0 4.5 %collective-permute-done.3 = bf16[128,4096]{1,0:T(8,128)(2,1)S(1)} collective-permute-done((bf16[128,4096]{1,0:T(8,128)(2,1)S(1)}, bf16[128,4096]{1,0:T(8,128)(2,1)S(1)}, u32[]{:S(2)}, u32[]{:S(2)}) %collective-permute-start.3) | collective-permute-done | bytes 1048608 | tf_op jit(solution)/shard_map/ppermute | solution.py:29
  57.5 0.3 copy_bitcast_fusion.1
  57.8 0.4 pad_maximum_fusion
  58.2 3.0 %gather_fusion.1 = bf16[128,128,128]{2,1,0:T(8,128)(2,1)} fusion(bf16[128,96,128]{2,0,1:T(8,128)(2,1)S(1)} %pad_maximum_fusion, s32[1024]{0:T(1024)S(1)} %pad_clamp_fusion), kind=kCustom, calls=%fused_computation.1 | custom fusion | bytes 8389120 | tf_op jit(solution)/shard_map/jit(_take)/gather | solution.py:96
  61.3 6.2 %fusion.5 = f32[32,128,128,1]{1,2,3,0:T(8,128)} fusion(bf16[32,4,128,128]{3,2,1,0:T(8,128)(2,1)} %param.14, bf16[32,4,128,128]{3,2,1,0:T(8,128)(2,1)} %bitcast.48, pred[32,4]{1,0:T(8,128)(4,1)S(1)} %copy.55), kind=kOutput, calls=%fused_computation.9 | convolution fusion | flops 538968064 | bytes 10485888 | tf_op jit(solution)/shard_map/kbsj,bsij->kbi/dot_general | solution.py:97
  67.4 0.0 copy-start.1
  67.4 0.0 copy-start.3
  67.4 0.0 copy-start.4
  67.4 2.0 %copy.60 = f32[128,4096]{1,0:T(8,128)S(1)} copy(f32[128,4096]{0,1:T(8,128)} %bitcast.51) | data formatting | bytes 4194304 | tf_op jit(solution)/shard_map/reshape | solution.py:99
  69.5 0.0 copy-done.1
  69.5 0.0 copy-done.3
  69.5 0.0 copy-done.4
  69.5 5.2 %fusion.4 = bf16[128,4096]{1,0:T(8,128)(2,1)} fusion(f32[128,4096]{1,0:T(8,128)} %param.10, f32[128,4096]{1,0:T(8,128)S(1)} %copy.60, f32[63,4096]{1,0:T(8,128)} %get-tuple-element.7, f32[1,4096]{1,0:T(1,128)S(1)} %broadcast_in_dim.42, f32[63,4096]{1,0:T(8,128)} %get-tuple-element.6, bf16[128,4096]{1,0:T(8,128)(2,1)S(1)} %bitcast.46, ...), kind=kOutput, calls=%fused_computation.8 | convolution fusion | flops 275939328 | bytes 9454720 | tf_op jit(solution)/shard_map/dot_general | solution.py:90
  74.7 0.5 broadcast.116
  75.2 2.6 %reduce = bf16[128,4096]{1,0:T(8,128)(2,1)S(1)} reduce(bf16[128,1,4096]{2,0,1:T(8,128)(2,1)} %bitcast.50, bf16[]{:T(256)} %broadcast.116), dimensions={1}, to_apply=%copy.61.reduce_sub_computation | reduce | bytes 2097154 | tf_op jit(solution)/shard_map/reshape | solution.py:103
  77.9 0.0 copy-start.5
  77.9 0.0 copy-start.2
  77.9 0.0 copy-start.7
  77.9 2.0 %reshape.120 = bf16[4,2,65536]{2,1,0:T(2,128)(2,1)} reshape(bf16[128,4096]{1,0:T(8,128)(2,1)S(1)} %reduce) | data formatting | bytes 2097152
  79.9 7.0 %all-to-all-start = ((bf16[4,2,65536]{2,1,0:T(2,128)(2,1)}), bf16[4,2,65536]{2,1,0:T(2,128)(2,1)S(1)}, u32[]{:S(2)}, u32[]{:S(2)}) async-start(bf16[4,2,65536]{2,1,0:T(2,128)(2,1)} %reshape.120), calls=%async_computation | async-start | bytes 2097152 | tf_op jit(solution)/shard_map/all_to_all | solution.py:102
  86.9 0.0 copy-done.5
  86.9 0.0 copy-done.2
  86.9 0.0 copy-done.7
  86.9 2.1 %fusion.11 = f32[120,128]{1,0:T(8,128)S(1)} fusion(bf16[128,4096]{1,0:T(8,128)(2,1)S(1)} %copy-done.2, f32[4096]{0:T(1024)S(1)} %copy-done.7, s32[4096]{0:T(1024)S(1)} %broadcast_subtract_fusion), kind=kOutput, calls=%fused_computation.17 | convolution fusion | flops 757006336 | bytes 1142784 | tf_op jit(solution)/shard_map/nz,nk->zk/dot_general | solution.py:110
  89.0 1.9 %collective-permute-start.5 = (f32[40,128]{1,0:T(8,128)S(1)}, f32[40,128]{1,0:T(8,128)S(1)}, u32[]{:S(2)}, u32[]{:S(2)}) collective-permute-start(f32[40,128]{1,0:T(8,128)S(1)} %get-tuple-element.12), channel_id=1, source_target_pairs={{1,0},{2,1},{3,2},{4,3},{5,4},{6,5},{7,6},{8,7},{9,8},{10,9},{11,1... | collective-permute-start | bytes 61448 | tf_op jit(solution)/shard_map/ppermute | solution.py:38
  91.0 2.4 %collective-permute-start.6 = (f32[40,128]{1,0:T(8,128)S(1)}, f32[40,128]{1,0:T(8,128)S(1)}, u32[]{:S(2)}, u32[]{:S(2)}) collective-permute-start(f32[40,128]{1,0:T(8,128)S(1)} %get-tuple-element.13), channel_id=1, source_target_pairs={{0,1},{1,2},{2,3},{3,4},{4,5},{5,6},{6,7},{7,8},{8,9},{9,10},{10,1... | collective-permute-start | bytes 61448 | tf_op jit(solution)/shard_map/ppermute | solution.py:38
  93.4 0.0 collective-permute-done.5
  93.4 3.6 %collective-permute-done.6 = f32[40,128]{1,0:T(8,128)S(1)} collective-permute-done((f32[40,128]{1,0:T(8,128)S(1)}, f32[40,128]{1,0:T(8,128)S(1)}, u32[]{:S(2)}, u32[]{:S(2)}) %collective-permute-start.6) | collective-permute-done | bytes 20512 | tf_op jit(solution)/shard_map/ppermute | solution.py:38
  97.0 0.6 fusion.26
  97.6 15.7 %all-to-all-done = bf16[4,2,65536]{2,1,0:T(2,128)(2,1)S(1)} async-done(((bf16[4,2,65536]{2,1,0:T(2,128)(2,1)}), bf16[4,2,65536]{2,1,0:T(2,128)(2,1)S(1)}, u32[]{:S(2)}, u32[]{:S(2)}) %all-to-all-start) | async-done | bytes 1048608 | tf_op jit(solution)/shard_map/all_to_all | solution.py:102
  113.3 0.9 reshape.121
  114.2 1.1 copy.64
  115.4 1.8 %copy.62 = bf16[32,4,4096]{2,1,0:T(4,128)(2,1)} copy(bf16[32,4,4096]{2,0,1:T(8,128)(2,1)S(1)} %bitcast.47) | data formatting | bytes 2097152
  (10 shorter events, 0.1 us)
Async XLA Ops:
  5.7 5.5 %copy-start.6 = (s32[32,4]{0,1:T(4,128)S(1)}, s32[32,4]{0,1:T(4,128)}, u32[]{:S(2)}) copy-start(s32[32,4]{0,1:T(4,128)} %param.15) | copy-start | bytes 1540
  6.0 12.8 %collective-permute-start = (bf16[32,1,4096]{2,0,1:T(8,128)(2,1)S(1)}, bf16[32,1,4096]{2,0,1:T(8,128)(2,1)S(1)}, u32[]{:S(2)}, u32[]{:S(2)}) collective-permute-start(bf16[32,1,4096]{2,0,1:T(8,128)(2,1)S(1)} %copy.66), channel_id=1, source_target_pairs={{0,8},{8,0},{16,24},{24,16},{1,9},{9,1},{17,25},{25,17},{2,10},{10... | collective-permute-start | bytes 786440 | tf_op jit(solution)/shard_map/ppermute | solution.py:78
  8.0 21.4 %collective-permute-start.1 = (bf16[32,1,4096]{2,0,1:T(8,128)(2,1)S(1)}, bf16[32,1,4096]{2,0,1:T(8,128)(2,1)S(1)}, u32[]{:S(2)}, u32[]{:S(2)}) collective-permute-start(bf16[32,1,4096]{2,0,1:T(8,128)(2,1)S(1)} %copy.67), channel_id=1, source_target_pairs={{0,16},{8,24},{16,0},{24,8},{1,17},{9,25},{17,1},{25,9},{2,18},{10... | collective-permute-start | bytes 786440 | tf_op jit(solution)/shard_map/ppermute | solution.py:78
  10.9 18.5 %collective-permute-start.2 = (bf16[32,1,4096]{2,0,1:T(8,128)(2,1)S(1)}, bf16[32,1,4096]{2,0,1:T(8,128)(2,1)S(1)}, u32[]{:S(2)}, u32[]{:S(2)}) collective-permute-start(bf16[32,1,4096]{2,0,1:T(8,128)(2,1)S(1)} %copy.68), channel_id=1, source_target_pairs={{0,24},{8,16},{16,8},{24,0},{1,25},{9,17},{17,9},{25,1},{2,26},{10... | collective-permute-start | bytes 786440 | tf_op jit(solution)/shard_map/ppermute | solution.py:78
  30.2 4.9 %copy-start = (bf16[4,32,4096]{2,1,0:T(8,128)(2,1)}, bf16[4,32,4096]{2,1,0:T(8,128)(2,1)S(1)}, u32[]{:S(2)}) copy-start(bf16[4,32,4096]{2,1,0:T(8,128)(2,1)S(1)} %gather_fusion) | copy-start | bytes 3145732
  30.2 22.6 %collective-permute-start.4 = (bf16[128,4096]{1,0:T(8,128)(2,1)S(1)}, bf16[128,4096]{1,0:T(8,128)(2,1)S(1)}, u32[]{:S(2)}, u32[]{:S(2)}) collective-permute-start(bf16[128,4096]{1,0:T(8,128)(2,1)S(1)} %bitcast.43), channel_id=1, source_target_pairs={{1,0},{2,1},{3,2},{4,3},{5,4},{6,5},{7,6},{8,7},{9,8},{10,9},{11,1... | collective-permute-start | bytes 3145736 | tf_op jit(solution)/shard_map/ppermute | solution.py:30
  32.1 25.4 %collective-permute-start.3 = (bf16[128,4096]{1,0:T(8,128)(2,1)S(1)}, bf16[128,4096]{1,0:T(8,128)(2,1)S(1)}, u32[]{:S(2)}, u32[]{:S(2)}) collective-permute-start(bf16[128,4096]{1,0:T(8,128)(2,1)S(1)} %bitcast.44), channel_id=1, source_target_pairs={{0,1},{1,2},{2,3},{3,4},{4,5},{5,6},{6,7},{7,8},{8,9},{9,10},{10,1... | collective-permute-start | bytes 3145736 | tf_op jit(solution)/shard_map/ppermute | solution.py:29
  67.4 2.0 %copy-start.1 = (bf16[4,32,4096]{2,1,0:T(8,128)(2,1)S(1)}, bf16[4,32,4096]{2,1,0:T(8,128)(2,1)}, u32[]{:S(2)}) copy-start(bf16[4,32,4096]{2,1,0:T(8,128)(2,1)} %copy-done) | copy-start | bytes 3145732
  67.4 2.0 %copy-start.3 = (f32[4096]{0:T(1024)S(1)}, f32[4096]{0:T(1024)}, u32[]{:S(2)}) copy-start(f32[4096]{0:T(1024)} %param.12) | copy-start | bytes 49156
  67.4 2.1 %copy-start.4 = (f32[4096]{0:T(1024)S(1)}, f32[4096]{0:T(1024)}, u32[]{:S(2)}) copy-start(f32[4096]{0:T(1024)} %param.13) | copy-start | bytes 49156
  77.9 9.0 %copy-start.5 = (s32[4096]{0:T(1024)S(1)}, s32[4096]{0:T(1024)}, u32[]{:S(2)}) copy-start(s32[4096]{0:T(1024)} %param.16) | copy-start | bytes 49156
  77.9 9.0 %copy-start.2 = (bf16[128,4096]{1,0:T(8,128)(2,1)S(1)}, bf16[128,4096]{1,0:T(8,128)(2,1)}, u32[]{:S(2)}) copy-start(bf16[128,4096]{1,0:T(8,128)(2,1)} %fusion.4) | copy-start | bytes 3145732
  77.9 9.0 %copy-start.7 = (f32[4096]{0:T(1024)S(1)}, f32[4096]{0:T(1024)}, u32[]{:S(2)}) copy-start(f32[4096]{0:T(1024)} %param.17) | copy-start | bytes 49156
  79.9 33.4 %all-to-all-start = ((bf16[4,2,65536]{2,1,0:T(2,128)(2,1)}), bf16[4,2,65536]{2,1,0:T(2,128)(2,1)S(1)}, u32[]{:S(2)}, u32[]{:S(2)}) async-start(bf16[4,2,65536]{2,1,0:T(2,128)(2,1)} %reshape.120), calls=%async_computation | async-start | bytes 2097152 | tf_op jit(solution)/shard_map/all_to_all | solution.py:102
  89.0 4.3 %collective-permute-start.5 = (f32[40,128]{1,0:T(8,128)S(1)}, f32[40,128]{1,0:T(8,128)S(1)}, u32[]{:S(2)}, u32[]{:S(2)}) collective-permute-start(f32[40,128]{1,0:T(8,128)S(1)} %get-tuple-element.12), channel_id=1, source_target_pairs={{1,0},{2,1},{3,2},{4,3},{5,4},{6,5},{7,6},{8,7},{9,8},{10,9},{11,1... | collective-permute-start | bytes 61448 | tf_op jit(solution)/shard_map/ppermute | solution.py:38
  91.0 6.0 %collective-permute-start.6 = (f32[40,128]{1,0:T(8,128)S(1)}, f32[40,128]{1,0:T(8,128)S(1)}, u32[]{:S(2)}, u32[]{:S(2)}) collective-permute-start(f32[40,128]{1,0:T(8,128)S(1)} %get-tuple-element.13), channel_id=1, source_target_pairs={{0,1},{1,2},{2,3},{3,4},{4,5},{5,6},{6,7},{7,8},{8,9},{9,10},{10,1... | collective-permute-start | bytes 61448 | tf_op jit(solution)/shard_map/ppermute | solution.py:38
